TPU v7x, 128 devices: a whole 4x4x4 slice. The times are simulated.
128 devices in a mesh: sub: 8 (over x, core), band: 16 (over z, y).
Axes of the slice: x: 4, y: 4, z: 4, core: 2. Of those that a mesh axis runs over, the one named last changes fastest.
Arguments:
- coeffs_in: float32 [32, 128, 1024], P('sub'), may hold values from -6 to 6
- basis: bfloat16 [224, 32], P('band'), may hold values from -0.375 to 0.375
- kernels: float32 [224, 9, 9], P('band'), may hold values from -0.625 to 0.625
- response: bfloat16 [8, 224], P(None, 'band'), may hold values from -1.5 to 1.5
- hs_image: bfloat16 [224, 32, 256], P('band', 'sub'), may hold values from -6 to 6
- ms_image: bfloat16 [8, 128, 1024], P(None, 'sub'), may hold values from -6 to 6
Outputs:
- coeffs: float32 [32, 128, 1024], P('sub')
All inputs are finite; a program needn't handle non-finite values.
Results may differ from a plain program's by a relative error of at most 0.0003.
The roundings to bfloat16 on the way count: a program that leaves them out, or rounds other values in their place, can miss the bound.
Values may be sent and summed in bfloat16 or wider, within the bound.
No kernel may reach another device: no remote copies, remote signals or barrier semaphores. Data moves between devices by JAX's collectives and lax.ppermute only.
A program may use at most 128 MiB of HBM per device.

v0:
```python
import jax
import jax.numpy as jnp
from jax import lax
from jax.sharding import PartitionSpec as P

ITERS = 2
step_scale = 0.15


def padded_2(cells, sides, width):
    for axis, dim in sides:
        count = lax.axis_size(axis)
        ends = count - 1
        head = lax.slice_in_dim(cells, 0, width, axis=dim)
        tail = lax.slice_in_dim(cells, cells.shape[dim] - width, cells.shape[dim], axis=dim)
        cells = jnp.concatenate(
            [
                lax.ppermute(tail, axis, [(i, (i + 1) % count) for i in range(ends)]),
                cells,
                lax.ppermute(head, axis, [((i + 1) % count, i) for i in range(ends)]),
            ],
            axis=dim,
        )
    return cells


def hs_gradient(rounded, basis, kernels, hs_image):
    chans, rows, width = rounded.shape
    bands = basis.shape[0]
    groups = rows // 4
    columns = width // 4
    mixed = jnp.dot(basis, rounded.reshape(chans, -1), preferred_element_type=jnp.float32).astype(
        jnp.bfloat16
    )
    mixed = mixed.reshape(bands, rows, width)
    extended = padded_2(mixed, (("sub", 1),), 4)
    padded = jnp.pad(extended, ((0, 0), (0, 0), (4, 4)))
    phases = padded.reshape(bands, groups + 2, 4, columns + 2, 4).transpose(0, 2, 4, 1, 3)
    blurred = jnp.zeros((bands, groups, columns), jnp.float32)
    for row_tap in range(9):
        row_step, row_phase = divmod(row_tap, 4)
        for col_tap in range(9):
            col_step, col_phase = divmod(col_tap, 4)
            window = phases[
                :, row_phase, col_phase, row_step : row_step + groups, col_step : col_step + columns
            ]
            blurred = blurred + kernels[:, row_tap, col_tap][:, None, None] * window
    misfit = hs_image.astype(jnp.float32) - blurred
    misfit_ext = padded_2(misfit, (("sub", 1),), 1)
    misfit_pad = jnp.pad(misfit_ext, ((0, 0), (0, 0), (1, 1)))
    outer = []
    for row_phase in range(4):
        inner = []
        for col_phase in range(4):
            total = jnp.zeros((bands, groups, columns), jnp.float32)
            for row_step in range(3):
                if 4 * row_step + row_phase > 8:
                    continue
                for col_step in range(3):
                    if 4 * col_step + col_phase > 8:
                        continue
                    weight = kernels[:, 4 * row_step + row_phase, 4 * col_step + col_phase][
                        :, None, None
                    ]
                    window = misfit_pad[
                        :,
                        2 - row_step : 2 - row_step + groups,
                        2 - col_step : 2 - col_step + columns,
                    ]
                    total = total + weight * window
            inner.append(total)
        outer.append(jnp.stack(inner, axis=1))
    back = jnp.stack(outer, axis=1).transpose(0, 3, 1, 4, 2).reshape(bands, rows * width)
    back = back.astype(jnp.bfloat16)
    grad = jnp.einsum("lk,lp->kp", basis, back, preferred_element_type=jnp.float32)
    return grad.reshape(chans, rows, width)


def ms_gradient(rounded, ms_rows, combined):
    chans, rows, width = rounded.shape
    sensors = ms_rows.shape[0]
    predicted = jnp.dot(combined, rounded.reshape(chans, -1), preferred_element_type=jnp.float32)
    ms_misfit = (ms_rows.reshape(sensors, -1).astype(jnp.float32) - predicted).astype(jnp.bfloat16)
    grad = jnp.einsum("mk,mp->kp", combined, ms_misfit, preferred_element_type=jnp.float32)
    return grad.reshape(chans, rows, width)


def per_device(coeffs_in, basis, kernels, response, hs_image, ms_image):
    partial_map = jnp.dot(response, basis, preferred_element_type=jnp.float32)
    combined = lax.psum(partial_map, "band").astype(jnp.bfloat16)
    current = coeffs_in
    for turn in range(ITERS):
        rounded = lax.all_to_all(
            current.astype(jnp.bfloat16), "sub", split_axis=1, concat_axis=0, tiled=True
        )
        hs_part = hs_gradient(rounded, basis, kernels, hs_image)
        hs_total = lax.psum(hs_part, "band")
        update = step_scale * (hs_total + ms_gradient(rounded, ms_image, combined))
        current = current + lax.all_to_all(update, "sub", split_axis=0, concat_axis=1, tiled=True)
    return current


def solution(mesh):
    return jax.shard_map(
        per_device,
        mesh=mesh,
        in_specs=(
            P("sub", None, None),
            P("band", None),
            P("band", None, None),
            P(None, "band"),
            P("band", "sub", None),
            P(None, "sub", None),
        ),
        out_specs=P("sub", None, None),
        check_vma=False,
    )
```

profile of v0, /device:TPU:1, one launch (start us, length us, event | category | flops | bytes accessed | tf_op | source)
XLA Modules:
  0.0 448.3 jit_solution(3410588063902400602)
XLA Ops:
  6.5 3.9 copy.459
  10.5 5.8 %all-to-all-start = ((bf16[4,128,1024]{2,0,1:T(4,128)(2,1)}), bf16[4,128,1024]{2,0,1:T(4,128)(2,1)S(1)}, u32[]{:S(2)}, u32[]{:S(2)}) async-start(bf16[4,128,1024]{2,0,1:T(4,128)(2,1)} %copy.459), calls=%async_computation | async-start | bytes 2097152 | tf_op jit(solution)/shard_map/all_to_all | solution.py:93
  19.6 11.8 %all-to-all-done = bf16[4,128,1024]{2,0,1:T(4,128)(2,1)S(1)} async-done(((bf16[4,128,1024]{2,0,1:T(4,128)(2,1)}), bf16[4,128,1024]{2,0,1:T(4,128)(2,1)S(1)}, u32[]{:S(2)}, u32[]{:S(2)}) %all-to-all-start) | async-done | bytes 1048608 | tf_op jit(solution)/shard_map/all_to_all | solution.py:93
  42.4 4.8 %copy.442 = bf16[14,24,1024]{0,2,1:T(8,128)(2,1)} copy(bf16[14,24,1024]{2,1,0:T(8,128)(2,1)S(1)} %pad_maximum_fusion) | data formatting | bytes 1376256
  47.2 7.5 %pad.14.clone = bf16[14,24,1032]{0,2,1:T(8,128)(2,1)} pad(bf16[14,24,1024]{0,2,1:T(8,128)(2,1)} %copy.442, bf16[]{:T(256)} %constant.4.clone.1), padding=0_0x0_0x4_4 | pad | bytes 1381634 | tf_op jit(solution)/shard_map/jit(_pad)/pad | solution.py:37
  54.7 11.1 %copy.392 = bf16[14,6,4,258,4]{3,1,0,4,2:T(8,128)(2,1)S(1)} copy(bf16[14,6,4,258,4]{0,4,3,2,1:T(4,128)(2,1)} %bitcast.1049) | data formatting | bytes 1387008 | tf_op jit(solution)/shard_map/reshape | solution.py:38
  65.8 3.8 convert_subtract_fusion.1
  86.3 4.9 %copy.413 = bf16[14,4,4,256,4]{0,4,3,2,1:T(4,128)(2,1)} copy(bf16[14,4,4,256,4]{3,1,4,2,0:T(4,128)(2,1)S(1)} %maximum_bitcast_fusion) | data formatting | bytes 917504 | tf_op jit(solution)/shard_map/convert_element_type | solution.py:74
  91.2 3.7 fusion.212
  98.9 35.0 %psum.22 = bf16[8,32]{1,0:T(8,128)(2,1)S(1)} all-reduce(f32[8,32]{1,0:T(8,128)S(1)} %fusion.213), channel_id=1, replica_groups=mesh['sub'=8,'band'=16] {'band'}, use_global_device_ids=true, to_apply=%region_1.2 | all-reduce | flops 256 | bytes 1536 | tf_op jit(solution)/shard_map/psum | solution.py:90
  138.5 49.5 %all-reduce.7.cloned.1.call-done = f32[32,16,1024]{2,1,0:T(8,128)} async-done(((f32[32,16,1024]{2,1,0:T(8,128)}), f32[32,16,1024]{2,1,0:T(8,128)}) %all-reduce.7.cloned.1.call-update) | async-done | bytes 2097168 | tf_op jit(solution)/shard_map/psum | solution.py:97
  189.9 32.4 %all_to_all.66 = f32[32,16,1024]{2,1,0:T(8,128)S(1)} all-to-all(f32[32,16,1024]{2,1,0:T(8,128)S(1)} %fusion.3), channel_id=1, replica_groups=mesh['sub'=8,'band'=16] {'sub'}, dimensions={0} | all-to-all | bytes 4194304 | tf_op jit(solution)/shard_map/all_to_all | solution.py:99
  225.7 18.5 %all_to_all.67 = bf16[4,128,1024]{2,0,1:T(4,128)(2,1)S(1)} all-to-all(bf16[4,128,1024]{2,0,1:T(4,128)(2,1)S(1)} %fusion.6), channel_id=1, replica_groups=mesh['sub'=8,'band'=16] {'sub'}, dimensions={1} | all-to-all | bytes 2097152 | tf_op jit(solution)/shard_map/all_to_all | solution.py:93
  246.9 3.1 collective-permute-start.4
  252.0 4.1 collective-permute-done.5
  256.4 4.8 %copy.443 = bf16[14,24,1024]{0,2,1:T(8,128)(2,1)} copy(bf16[14,24,1024]{2,1,0:T(8,128)(2,1)S(1)} %pad_maximum_fusion.1) | data formatting | bytes 1376256
  261.2 7.5 %pad.16.clone = bf16[14,24,1032]{0,2,1:T(8,128)(2,1)} pad(bf16[14,24,1024]{0,2,1:T(8,128)(2,1)} %copy.443, bf16[]{:T(256)} %constant.4.clone.1), padding=0_0x0_0x4_4 | pad | bytes 1381634 | tf_op jit(solution)/shard_map/jit(_pad)/pad | solution.py:37
  268.7 11.1 %copy.418 = bf16[14,6,4,258,4]{3,1,0,4,2:T(8,128)(2,1)S(1)} copy(bf16[14,6,4,258,4]{0,4,3,2,1:T(4,128)(2,1)} %bitcast.1048) | data formatting | bytes 1387008 | tf_op jit(solution)/shard_map/reshape | solution.py:38
  280.0 4.2 convert_subtract_fusion
  301.1 4.9 %copy.439 = bf16[14,4,4,256,4]{0,4,3,2,1:T(4,128)(2,1)} copy(bf16[14,4,4,256,4]{3,1,4,2,0:T(4,128)(2,1)S(1)} %maximum_bitcast_fusion.1) | data formatting | bytes 917504 | tf_op jit(solution)/shard_map/convert_element_type | solution.py:74
  306.0 3.7 fusion.214
  316.4 4.1 copy.452
  320.5 79.2 %all-reduce.9.cloned.1.call-done = f32[32,16,1024]{2,1,0:T(8,128)} async-done(((f32[32,16,1024]{2,1,0:T(8,128)}), f32[32,16,1024]{2,1,0:T(8,128)}) %all-reduce.9.cloned.1.call-update) | async-done | bytes 2097168 | tf_op jit(solution)/shard_map/psum | solution.py:97
  402.3 32.5 %all_to_all.68 = f32[32,16,1024]{2,1,0:T(8,128)S(1)} all-to-all(f32[32,16,1024]{2,1,0:T(8,128)S(1)} %fusion.2), channel_id=1, replica_groups=mesh['sub'=8,'band'=16] {'sub'}, dimensions={0} | all-to-all | bytes 4194304 | tf_op jit(solution)/shard_map/all_to_all | solution.py:99
  (266 shorter events, 81.1 us)
Async XLA Ops:
  10.5 20.9 %all-to-all-start = ((bf16[4,128,1024]{2,0,1:T(4,128)(2,1)}), bf16[4,128,1024]{2,0,1:T(4,128)(2,1)S(1)}, u32[]{:S(2)}, u32[]{:S(2)}) async-start(bf16[4,128,1024]{2,0,1:T(4,128)(2,1)} %copy.459), calls=%async_computation | async-start | bytes 2097152 | tf_op jit(solution)/shard_map/all_to_all | solution.py:93
  16.3 171.7 %all-reduce.7.cloned.1.call-start = ((), (), s32[]{:S(2)}) async-start(), calls=%async_computation.4 | async-start | bytes 4194304 | tf_op jit(solution)/shard_map/psum | solution.py:97
  17.3 66.2 %copy-start.22 = (f32[14]{0:T(128)}, f32[14]{0:T(128)S(1)}, u32[]{:S(2)}) copy-start(f32[14]{0:T(128)S(1)} %get-tuple-element.23) | copy-start | bytes 172
  18.4 65.2 %copy-start.38 = (f32[14]{0:T(128)}, f32[14]{0:T(128)S(1)}, u32[]{:S(2)}) copy-start(f32[14]{0:T(128)S(1)} %get-tuple-element.28) | copy-start | bytes 172
  18.4 66.7 %copy-start.24 = (f32[14]{0:T(128)}, f32[14]{0:T(128)S(1)}, u32[]{:S(2)}) copy-start(f32[14]{0:T(128)S(1)} %get-tuple-element.27) | copy-start | bytes 172
  18.4 66.7 %copy-start.26 = (f32[14]{0:T(128)}, f32[14]{0:T(128)S(1)}, u32[]{:S(2)}) copy-start(f32[14]{0:T(128)S(1)} %get-tuple-element.31) | copy-start | bytes 172
  18.4 67.0 %copy-start.12 = (f32[14]{0:T(128)}, f32[14]{0:T(128)S(1)}, u32[]{:S(2)}) copy-start(f32[14]{0:T(128)S(1)} %get-tuple-element.26) | copy-start | bytes 172
  18.4 67.0 %copy-start.14 = (f32[14]{0:T(128)}, f32[14]{0:T(128)S(1)}, u32[]{:S(2)}) copy-start(f32[14]{0:T(128)S(1)} %get-tuple-element.30) | copy-start | bytes 172
  19.5 65.2 %copy-start.16 = (f32[14]{0:T(128)}, f32[14]{0:T(128)S(1)}, u32[]{:S(2)}) copy-start(f32[14]{0:T(128)S(1)} %get-tuple-element.51) | copy-start | bytes 172
  19.5 65.2 %copy-start.18 = (f32[14]{0:T(128)}, f32[14]{0:T(128)S(1)}, u32[]{:S(2)}) copy-start(f32[14]{0:T(128)S(1)} %get-tuple-element.55) | copy-start | bytes 172
  19.5 65.2 %copy-start.20 = (f32[14]{0:T(128)}, f32[14]{0:T(128)S(1)}, u32[]{:S(2)}) copy-start(f32[14]{0:T(128)S(1)} %get-tuple-element.59) | copy-start | bytes 172
  19.5 65.4 %copy-start.10 = (f32[14]{0:T(128)}, f32[14]{0:T(128)S(1)}, u32[]{:S(2)}) copy-start(f32[14]{0:T(128)S(1)} %get-tuple-element.57) | copy-start | bytes 172
  19.5 65.6 %copy-start.36 = (f32[14]{0:T(128)}, f32[14]{0:T(128)S(1)}, u32[]{:S(2)}) copy-start(f32[14]{0:T(128)S(1)} %get-tuple-element.60) | copy-start | bytes 172
  19.5 65.9 %copy-start.28 = (f32[14]{0:T(128)}, f32[14]{0:T(128)S(1)}, u32[]{:S(2)}) copy-start(f32[14]{0:T(128)S(1)} %get-tuple-element.52) | copy-start | bytes 172
  19.5 65.9 %copy-start.30 = (f32[14]{0:T(128)}, f32[14]{0:T(128)S(1)}, u32[]{:S(2)}) copy-start(f32[14]{0:T(128)S(1)} %get-tuple-element.56) | copy-start | bytes 172
  33.0 6.9 %collective-permute-start = (bf16[14,4,1024]{2,1,0:T(4,128)(2,1)S(1)}, bf16[14,4,1024]{2,1,0:T(4,128)(2,1)S(1)}, u32[]{:S(2)}, u32[]{:S(2)}) collective-permute-start(bf16[14,4,1024]{2,1,0:T(4,128)(2,1)S(1)} %get-tuple-element.88), channel_id=1, source_target_pairs={{0,16},{16,32},{32,48},{48,64},{64,80},{80,96},{96,112},{1,17},{17... | collective-permute-start | bytes 344072 | tf_op jit(solution)/shard_map/ppermute | solution.py:18
  36.0 6.1 %collective-permute-start.1 = (bf16[14,4,1024]{2,1,0:T(4,128)(2,1)S(1)}, bf16[14,4,1024]{2,1,0:T(4,128)(2,1)S(1)}, u32[]{:S(2)}, u32[]{:S(2)}) collective-permute-start(bf16[14,4,1024]{2,1,0:T(4,128)(2,1)S(1)} %get-tuple-element.89), channel_id=1, source_target_pairs={{16,0},{32,16},{48,32},{64,48},{80,64},{96,80},{112,96},{17,1},{33... | collective-permute-start | bytes 344072 | tf_op jit(solution)/shard_map/ppermute | solution.py:20
  69.6 4.9 %collective-permute-start.2 = (f32[14,1,256]{2,1,0:T(1,128)S(1)}, f32[14,1,256]{2,1,0:T(1,128)S(1)}, u32[]{:S(2)}, u32[]{:S(2)}) collective-permute-start(f32[14,1,256]{2,1,0:T(1,128)S(1)} %get-tuple-element.108), channel_id=1, source_target_pairs={{0,16},{16,32},{32,48},{48,64},{64,80},{80,96},{96,112},{1,17},{17... | collective-permute-start | bytes 43016 | tf_op jit(solution)/shard_map/ppermute | solution.py:18
  71.5 5.0 %collective-permute-start.3 = (f32[14,1,256]{2,1,0:T(1,128)S(1)}, f32[14,1,256]{2,1,0:T(1,128)S(1)}, u32[]{:S(2)}, u32[]{:S(2)}) collective-permute-start(f32[14,1,256]{2,1,0:T(1,128)S(1)} %get-tuple-element.109), channel_id=1, source_target_pairs={{16,0},{32,16},{48,32},{64,48},{80,64},{96,80},{112,96},{17,1},{33... | collective-permute-start | bytes 43016 | tf_op jit(solution)/shard_map/ppermute | solution.py:20
  97.4 302.2 %all-reduce.9.cloned.1.call-start = ((), (), s32[]{:S(2)}) async-start(), calls=%async_computation.5 | async-start | bytes 4194304 | tf_op jit(solution)/shard_map/psum | solution.py:97
  246.9 5.1 %collective-permute-start.4 = (bf16[14,4,1024]{2,1,0:T(4,128)(2,1)S(1)}, bf16[14,4,1024]{2,1,0:T(4,128)(2,1)S(1)}, u32[]{:S(2)}, u32[]{:S(2)}) collective-permute-start(bf16[14,4,1024]{2,1,0:T(4,128)(2,1)S(1)} %get-tuple-element.86), channel_id=1, source_target_pairs={{0,16},{16,32},{32,48},{48,64},{64,80},{80,96},{96,112},{1,17},{17... | collective-permute-start | bytes 344072 | tf_op jit(solution)/shard_map/ppermute | solution.py:18
  250.0 6.1 %collective-permute-start.5 = (bf16[14,4,1024]{2,1,0:T(4,128)(2,1)S(1)}, bf16[14,4,1024]{2,1,0:T(4,128)(2,1)S(1)}, u32[]{:S(2)}, u32[]{:S(2)}) collective-permute-start(bf16[14,4,1024]{2,1,0:T(4,128)(2,1)S(1)} %get-tuple-element.87), channel_id=1, source_target_pairs={{16,0},{32,16},{48,32},{64,48},{80,64},{96,80},{112,96},{17,1},{33... | collective-permute-start | bytes 344072 | tf_op jit(solution)/shard_map/ppermute | solution.py:20
  284.4 4.6 %collective-permute-start.6 = (f32[14,1,256]{2,1,0:T(1,128)S(1)}, f32[14,1,256]{2,1,0:T(1,128)S(1)}, u32[]{:S(2)}, u32[]{:S(2)}) collective-permute-start(f32[14,1,256]{2,1,0:T(1,128)S(1)} %get-tuple-element.106), channel_id=1, source_target_pairs={{0,16},{16,32},{32,48},{48,64},{64,80},{80,96},{96,112},{1,17},{17... | collective-permute-start | bytes 43016 | tf_op jit(solution)/shard_map/ppermute | solution.py:18
  286.3 5.0 %collective-permute-start.7 = (f32[14,1,256]{2,1,0:T(1,128)S(1)}, f32[14,1,256]{2,1,0:T(1,128)S(1)}, u32[]{:S(2)}, u32[]{:S(2)}) collective-permute-start(f32[14,1,256]{2,1,0:T(1,128)S(1)} %get-tuple-element.107), channel_id=1, source_target_pairs={{16,0},{32,16},{48,32},{64,48},{80,64},{96,80},{112,96},{17,1},{33... | collective-permute-start | bytes 43016 | tf_op jit(solution)/shard_map/ppermute | solution.py:20
  (76 other events, 2264.0 us)
Sparse Core Ops, SparseCore 0:
  97.6 90.3 all-reduce.6
  312.4 87.1 all-reduce.8
where the time goes:
time: 457 us; the launch traced here: 448 us
  waiting for transfers between devices  151 us (33%)
  blocking collectives  118 us (26%)
  local copies, waits for them, and re-layouts  89.6 us (20%)
  other arithmetic  35.7 us (8%)
  starting transfers between devices  25.1 us (5%)
  between operations  15.4 us (3%)
  matrix products  12.7 us (3%)
    psum x2, waiting for transfers between devices, per_device(): hs_total = lax.psum(hs_part, 'band')  129 us
    all_to_all x2, blocking collectives, per_device(): lax.all_to_all(update, 'sub', split_axis=0, concat_axis=1, tiled=True)  64.9 us
    psum x1, blocking collectives, per_device(): combined = lax.psum(partial_map, 'band').astype(jnp.bfloat16)  35 us
    unnamed x190, local copies, waits for them, and re-layouts  31.5 us
    reshape x2, local copies, waits for them, and re-layouts, hs_gradient(): padded.reshape(bands, groups + 2, 4, columns + 2, 4)  22.2 us
    all_to_all x1, blocking collectives, per_device(): lax.all_to_all(current.astype(jnp.bfloat16), 'sub', split_axis=1, concat_...  18.5 us
    another operation x24, other arithmetic, hs_gradient(): outer.append(jnp.stack(inner, axis=1))  16.7 us
    pad x2, local copies, waits for them, and re-layouts, hs_gradient(): padded = jnp.pad(extended, ((0, 0), (0, 0), (4, 4)))  15 us
  transfers between devices with their start and end apart: 11, of which 7 were waited for; matrix products, arithmetic and copies ran while one was open for 4% of the time, Pallas kernels for 0%

commit v1 on v0

--- a/solution.py
+++ b/solution.py
@@ -5,6 +5,16 @@
 
 ITERS = 2
 step_scale = 0.15
+
+
+def measure_the_patch(x0, mesh_dim):
+    n_chips = lax.axis_size(mesh_dim)
+    carry, prior = (x0, 0)
+    while 1 << prior < n_chips:
+        z_new = lax.ppermute(carry, mesh_dim, perm=[(c, c ^ 1 << prior) for c in range(n_chips)])
+        carry = carry + z_new
+        prior = prior + 1
+    return carry
 
 
 def padded_2(cells, sides, width):
@@ -94,7 +104,7 @@
             current.astype(jnp.bfloat16), "sub", split_axis=1, concat_axis=0, tiled=True
         )
         hs_part = hs_gradient(rounded, basis, kernels, hs_image)
-        hs_total = lax.psum(hs_part, "band")
+        hs_total = measure_the_patch(hs_part, "band")
         update = step_scale * (hs_total + ms_gradient(rounded, ms_image, combined))
         current = current + lax.all_to_all(update, "sub", split_axis=0, concat_axis=1, tiled=True)
     return current

time: 457 us -> 650 us (1.42)
  waiting for transfers between devices: 151 us -> 346 us
  starting transfers between devices: 25.1 us -> 39.9 us
  between operations: 15.4 us -> 1.98 us
  other arithmetic: 35.7 us -> 42.2 us
    ppermute x0 -> x8, waiting for transfers between devices: none -> 324 us  [measure_the_patch(): lax.ppermute(carry, mesh_dim, perm=[(c, c ^ 1 << prior) for c in range(n_...]
    psum x2 -> x0, waiting for transfers between devices: 129 us -> none  [per_device(): hs_total = lax.psum(hs_part, 'band')]
    ppermute x0 -> x8, starting transfers between devices: none -> 15 us  [measure_the_patch(): lax.ppermute(carry, mesh_dim, perm=[(c, c ^ 1 << prior) for c in range(n_...]
  transfers between devices with their start and end apart: 11 -> 17, of which waited for: 7 -> 13; matrix products, arithmetic and copies ran while one was open for 4% -> 2% of each run, Pallas kernels for 0% -> 0%
where the time goes in v1:
time: 650 us; the launch traced here: 641 us
  waiting for transfers between devices  346 us (53%)
  blocking collectives  114 us (18%)
  local copies, waits for them, and re-layouts  83.5 us (13%)
  other arithmetic  42.2 us (6%)
  starting transfers between devices  39.9 us (6%)
  matrix products  12.8 us (2%)
    ppermute x8, waiting for transfers between devices, measure_the_patch(): lax.ppermute(carry, mesh_dim, perm=[(c, c ^ 1 << prior) for c in range(n_...  324 us
    all_to_all x2, blocking collectives, per_device(): lax.all_to_all(update, 'sub', split_axis=0, concat_axis=1, tiled=True)  63.6 us
    psum x1, blocking collectives, per_device(): combined = lax.psum(partial_map, 'band').astype(jnp.bfloat16)  31.9 us
    unnamed x190, local copies, waits for them, and re-layouts  25.4 us
    reshape x2, local copies, waits for them, and re-layouts, hs_gradient(): padded.reshape(bands, groups + 2, 4, columns + 2, 4)  22.2 us
    all_to_all x1, blocking collectives, per_device(): lax.all_to_all(current.astype(jnp.bfloat16), 'sub', split_axis=1, concat_...  18.5 us
    another operation x24, other arithmetic, hs_gradient(): outer.append(jnp.stack(inner, axis=1))  16.3 us
    ppermute x8, starting transfers between devices, measure_the_patch(): lax.ppermute(carry, mesh_dim, perm=[(c, c ^ 1 << prior) for c in range(n_...  15 us
  transfers between devices with their start and end apart: 17, of which 13 were waited for; matrix products, arithmetic and copies ran while one was open for 2% of the time, Pallas kernels for 0%

profile of v1, /device:TPU:1, one launch (start us, length us, event | category | flops | bytes accessed | tf_op | source)
XLA Modules:
  0.0 640.9 jit_solution(12551910427168771347)
XLA Ops:
  3.9 5.8 all-to-all-start
  13.0 11.8 %all-to-all-done = bf16[4,128,1024]{2,0,1:T(4,128)(2,1)S(1)} async-done(((bf16[4,128,1024]{2,0,1:T(4,128)(2,1)}), bf16[4,128,1024]{2,0,1:T(4,128)(2,1)S(1)}, u32[]{:S(2)}, u32[]{:S(2)}) %all-to-all-start) | async-done | bytes 1048608 | tf_op jit(solution)/shard_map/all_to_all | solution.py:103
  35.9 4.8 copy.442
  40.7 7.5 %pad.14.clone = bf16[14,24,1032]{0,2,1:T(8,128)(2,1)} pad(bf16[14,24,1024]{0,2,1:T(8,128)(2,1)} %copy.442, bf16[]{:T(256)} %constant.4.clone.1), padding=0_0x0_0x4_4 | pad | bytes 1381634 | tf_op jit(solution)/shard_map/jit(_pad)/pad | solution.py:47
  48.1 11.1 %copy.392 = bf16[14,6,4,258,4]{3,1,0,4,2:T(8,128)(2,1)S(1)} copy(bf16[14,6,4,258,4]{0,4,3,2,1:T(4,128)(2,1)} %bitcast.1051) | data formatting | bytes 1387008 | tf_op jit(solution)/shard_map/reshape | solution.py:48
  79.6 4.9 copy.413
  90.8 45.1 %collective-permute-done.4 = f32[32,16,1024]{2,1,0:T(8,128)S(1)} collective-permute-done((f32[32,16,1024]{2,1,0:T(8,128)S(1)}, f32[32,16,1024]{2,1,0:T(8,128)S(1)}, u32[]{:S(2)}, u32[]{:S(2)}) %collective-permute-start.4) | collective-permute-done | bytes 2097184 | tf_op jit(solution)/shard_map/ppermute | solution.py:14
  139.4 46.1 %collective-permute-done.5 = f32[32,16,1024]{2,1,0:T(8,128)S(1)} collective-permute-done((f32[32,16,1024]{2,1,0:T(8,128)S(1)}, f32[32,16,1024]{2,1,0:T(8,128)S(1)}, u32[]{:S(2)}, u32[]{:S(2)}) %collective-permute-start.5) | collective-permute-done | bytes 2097184 | tf_op jit(solution)/shard_map/ppermute | solution.py:14
  187.8 45.4 %collective-permute-done.6 = f32[32,16,1024]{2,1,0:T(8,128)S(1)} collective-permute-done((f32[32,16,1024]{2,1,0:T(8,128)S(1)}, f32[32,16,1024]{2,1,0:T(8,128)S(1)}, u32[]{:S(2)}, u32[]{:S(2)}) %collective-permute-start.6) | collective-permute-done | bytes 2097184 | tf_op jit(solution)/shard_map/ppermute | solution.py:14
  238.6 31.9 %psum.7 = bf16[8,32]{1,0:T(8,128)(2,1)S(1)} all-reduce(f32[8,32]{1,0:T(8,128)S(1)} %fusion.213), channel_id=1, replica_groups=mesh['sub'=8,'band'=16] {'band'}, use_global_device_ids=true, to_apply=%region_0.0 | all-reduce | flops 256 | bytes 1536 | tf_op jit(solution)/shard_map/psum | solution.py:100
  275.2 8.6 %collective-permute-done.7 = f32[32,16,1024]{2,1,0:T(8,128)} collective-permute-done((f32[32,16,1024]{2,1,0:T(8,128)}, f32[32,16,1024]{2,1,0:T(8,128)}, u32[]{:S(2)}, u32[]{:S(2)}) %collective-permute-start.7) | collective-permute-done | bytes 2097184 | tf_op jit(solution)/shard_map/ppermute | solution.py:14
  286.7 31.7 %all_to_all.66 = f32[32,16,1024]{2,1,0:T(8,128)S(1)} all-to-all(f32[32,16,1024]{2,1,0:T(8,128)S(1)} %fusion.3), channel_id=1, replica_groups=mesh['sub'=8,'band'=16] {'sub'}, dimensions={0} | all-to-all | bytes 4194304 | tf_op jit(solution)/shard_map/all_to_all | solution.py:109
  321.8 18.5 %all_to_all.67 = bf16[4,128,1024]{2,0,1:T(4,128)(2,1)S(1)} all-to-all(bf16[4,128,1024]{2,0,1:T(4,128)(2,1)S(1)} %fusion.6), channel_id=1, replica_groups=mesh['sub'=8,'band'=16] {'sub'}, dimensions={1} | all-to-all | bytes 2097152 | tf_op jit(solution)/shard_map/all_to_all | solution.py:103
  348.0 4.1 collective-permute-done.9
  352.5 4.8 copy.443
  357.3 7.5 %pad.16.clone = bf16[14,24,1032]{0,2,1:T(8,128)(2,1)} pad(bf16[14,24,1024]{0,2,1:T(8,128)(2,1)} %copy.443, bf16[]{:T(256)} %constant.4.clone.1), padding=0_0x0_0x4_4 | pad | bytes 1381634 | tf_op jit(solution)/shard_map/jit(_pad)/pad | solution.py:47
  364.7 11.1 %copy.418 = bf16[14,6,4,258,4]{3,1,0,4,2:T(8,128)(2,1)S(1)} copy(bf16[14,6,4,258,4]{0,4,3,2,1:T(4,128)(2,1)} %bitcast.1050) | data formatting | bytes 1387008 | tf_op jit(solution)/shard_map/reshape | solution.py:48
  376.1 4.2 convert_subtract_fusion
  397.0 4.9 copy.439
  407.4 45.9 %collective-permute-done.12 = f32[32,16,1024]{2,1,0:T(8,128)S(1)} collective-permute-done((f32[32,16,1024]{2,1,0:T(8,128)S(1)}, f32[32,16,1024]{2,1,0:T(8,128)S(1)}, u32[]{:S(2)}, u32[]{:S(2)}) %collective-permute-start.12) | collective-permute-done | bytes 2097184 | tf_op jit(solution)/shard_map/ppermute | solution.py:14
  455.9 47.0 %collective-permute-done.13 = f32[32,16,1024]{2,1,0:T(8,128)S(1)} collective-permute-done((f32[32,16,1024]{2,1,0:T(8,128)S(1)}, f32[32,16,1024]{2,1,0:T(8,128)S(1)}, u32[]{:S(2)}, u32[]{:S(2)}) %collective-permute-start.13) | collective-permute-done | bytes 2097184 | tf_op jit(solution)/shard_map/ppermute | solution.py:14
  503.7 46.5 %collective-permute-done.14 = f32[32,16,1024]{2,1,0:T(8,128)S(1)} collective-permute-done((f32[32,16,1024]{2,1,0:T(8,128)S(1)}, f32[32,16,1024]{2,1,0:T(8,128)S(1)}, u32[]{:S(2)}, u32[]{:S(2)}) %collective-permute-start.14) | collective-permute-done | bytes 2097184 | tf_op jit(solution)/shard_map/ppermute | solution.py:14
  560.5 39.0 %collective-permute-done.15 = f32[32,16,1024]{2,1,0:T(8,128)} collective-permute-done((f32[32,16,1024]{2,1,0:T(8,128)}, f32[32,16,1024]{2,1,0:T(8,128)}, u32[]{:S(2)}, u32[]{:S(2)}) %collective-permute-start.15) | collective-permute-done | bytes 2097184 | tf_op jit(solution)/shard_map/ppermute | solution.py:14
  602.4 31.9 %all_to_all.68 = f32[32,16,1024]{2,1,0:T(8,128)S(1)} all-to-all(f32[32,16,1024]{2,1,0:T(8,128)S(1)} %fusion.2), channel_id=1, replica_groups=mesh['sub'=8,'band'=16] {'sub'}, dimensions={0} | all-to-all | bytes 4194304 | tf_op jit(solution)/shard_map/all_to_all | solution.py:109
  (282 shorter events, 118.8 us)
Async XLA Ops:
  3.9 20.9 %all-to-all-start = ((bf16[4,128,1024]{2,0,1:T(4,128)(2,1)}), bf16[4,128,1024]{2,0,1:T(4,128)(2,1)S(1)}, u32[]{:S(2)}, u32[]{:S(2)}) async-start(bf16[4,128,1024]{2,0,1:T(4,128)(2,1)} %copy.459), calls=%async_computation | async-start | bytes 2097152 | tf_op jit(solution)/shard_map/all_to_all | solution.py:103
  10.7 66.1 %copy-start.22 = (f32[14]{0:T(128)}, f32[14]{0:T(128)S(1)}, u32[]{:S(2)}) copy-start(f32[14]{0:T(128)S(1)} %get-tuple-element.23) | copy-start | bytes 172
  11.9 66.6 %copy-start.24 = (f32[14]{0:T(128)}, f32[14]{0:T(128)S(1)}, u32[]{:S(2)}) copy-start(f32[14]{0:T(128)S(1)} %get-tuple-element.27) | copy-start | bytes 172
  11.9 66.6 %copy-start.26 = (f32[14]{0:T(128)}, f32[14]{0:T(128)S(1)}, u32[]{:S(2)}) copy-start(f32[14]{0:T(128)S(1)} %get-tuple-element.31) | copy-start | bytes 172
  11.9 66.8 %copy-start.12 = (f32[14]{0:T(128)}, f32[14]{0:T(128)S(1)}, u32[]{:S(2)}) copy-start(f32[14]{0:T(128)S(1)} %get-tuple-element.26) | copy-start | bytes 172
  11.9 66.8 %copy-start.14 = (f32[14]{0:T(128)}, f32[14]{0:T(128)S(1)}, u32[]{:S(2)}) copy-start(f32[14]{0:T(128)S(1)} %get-tuple-element.30) | copy-start | bytes 172
  13.0 65.7 %copy-start.28 = (f32[14]{0:T(128)}, f32[14]{0:T(128)S(1)}, u32[]{:S(2)}) copy-start(f32[14]{0:T(128)S(1)} %get-tuple-element.52) | copy-start | bytes 172
  13.0 65.7 %copy-start.30 = (f32[14]{0:T(128)}, f32[14]{0:T(128)S(1)}, u32[]{:S(2)}) copy-start(f32[14]{0:T(128)S(1)} %get-tuple-element.56) | copy-start | bytes 172
  26.5 6.8 %collective-permute-start = (bf16[14,4,1024]{2,1,0:T(4,128)(2,1)S(1)}, bf16[14,4,1024]{2,1,0:T(4,128)(2,1)S(1)}, u32[]{:S(2)}, u32[]{:S(2)}) collective-permute-start(bf16[14,4,1024]{2,1,0:T(4,128)(2,1)S(1)} %get-tuple-element.88), channel_id=1, source_target_pairs={{0,16},{16,32},{32,48},{48,64},{64,80},{80,96},{96,112},{1,17},{17... | collective-permute-start | bytes 344072 | tf_op jit(solution)/shard_map/ppermute | solution.py:28
  29.4 6.1 collective-permute-start.1
  63.1 4.5 collective-permute-start.2
  65.0 5.0 collective-permute-start.3
  89.4 46.4 %collective-permute-start.4 = (f32[32,16,1024]{2,1,0:T(8,128)S(1)}, f32[32,16,1024]{2,1,0:T(8,128)S(1)}, u32[]{:S(2)}, u32[]{:S(2)}) collective-permute-start(f32[32,16,1024]{2,1,0:T(8,128)S(1)} %bitcast.1060), channel_id=1, source_target_pairs={{0,1},{1,0},{2,3},{3,2},{4,5},{5,4},{6,7},{7,6},{8,9},{9,8},{10,11... | collective-permute-start | bytes 6291464 | tf_op jit(solution)/shard_map/ppermute | solution.py:14
  136.4 49.1 %collective-permute-start.5 = (f32[32,16,1024]{2,1,0:T(8,128)S(1)}, f32[32,16,1024]{2,1,0:T(8,128)S(1)}, u32[]{:S(2)}, u32[]{:S(2)}) collective-permute-start(f32[32,16,1024]{2,1,0:T(8,128)S(1)} %bitcast_add_fusion.5), channel_id=1, source_target_pairs={{0,2},{1,3},{2,0},{3,1},{4,6},{5,7},{6,4},{7,5},{8,10},{9,11},{10,... | collective-permute-start | bytes 6291464 | tf_op jit(solution)/shard_map/ppermute | solution.py:14
  186.0 47.1 %collective-permute-start.6 = (f32[32,16,1024]{2,1,0:T(8,128)S(1)}, f32[32,16,1024]{2,1,0:T(8,128)S(1)}, u32[]{:S(2)}, u32[]{:S(2)}) collective-permute-start(f32[32,16,1024]{2,1,0:T(8,128)S(1)} %add.1062), channel_id=1, source_target_pairs={{0,4},{1,5},{2,6},{3,7},{4,0},{5,1},{6,2},{7,3},{8,12},{9,13},{10,... | collective-permute-start | bytes 6291464 | tf_op jit(solution)/shard_map/ppermute | solution.py:14
  234.9 48.9 %collective-permute-start.7 = (f32[32,16,1024]{2,1,0:T(8,128)}, f32[32,16,1024]{2,1,0:T(8,128)}, u32[]{:S(2)}, u32[]{:S(2)}) collective-permute-start(f32[32,16,1024]{2,1,0:T(8,128)} %add.1063), channel_id=1, source_target_pairs={{0,8},{1,9},{2,10},{3,11},{4,12},{5,13},{6,14},{7,15},{8,0},{9,1},... | collective-permute-start | bytes 6291464 | tf_op jit(solution)/shard_map/ppermute | solution.py:14
  342.9 5.1 collective-permute-start.8
  346.0 6.1 collective-permute-start.9
  380.5 4.8 collective-permute-start.10
  382.4 5.0 collective-permute-start.11
  406.8 46.4 %collective-permute-start.12 = (f32[32,16,1024]{2,1,0:T(8,128)S(1)}, f32[32,16,1024]{2,1,0:T(8,128)S(1)}, u32[]{:S(2)}, u32[]{:S(2)}) collective-permute-start(f32[32,16,1024]{2,1,0:T(8,128)S(1)} %bitcast.1061), channel_id=1, source_target_pairs={{0,1},{1,0},{2,3},{3,2},{4,5},{5,4},{6,7},{7,6},{8,9},{9,8},{10,11... | collective-permute-start | bytes 6291464 | tf_op jit(solution)/shard_map/ppermute | solution.py:14
  453.8 49.1 %collective-permute-start.13 = (f32[32,16,1024]{2,1,0:T(8,128)S(1)}, f32[32,16,1024]{2,1,0:T(8,128)S(1)}, u32[]{:S(2)}, u32[]{:S(2)}) collective-permute-start(f32[32,16,1024]{2,1,0:T(8,128)S(1)} %bitcast_add_fusion.4), channel_id=1, source_target_pairs={{0,2},{1,3},{2,0},{3,1},{4,6},{5,7},{6,4},{7,5},{8,10},{9,11},{10,... | collective-permute-start | bytes 6291464 | tf_op jit(solution)/shard_map/ppermute | solution.py:14
  503.5 46.7 %collective-permute-start.14 = (f32[32,16,1024]{2,1,0:T(8,128)S(1)}, f32[32,16,1024]{2,1,0:T(8,128)S(1)}, u32[]{:S(2)}, u32[]{:S(2)}) collective-permute-start(f32[32,16,1024]{2,1,0:T(8,128)S(1)} %add.1213), channel_id=1, source_target_pairs={{0,4},{1,5},{2,6},{3,7},{4,0},{5,1},{6,2},{7,3},{8,12},{9,13},{10,... | collective-permute-start | bytes 6291464 | tf_op jit(solution)/shard_map/ppermute | solution.py:14
  552.0 47.5 %collective-permute-start.15 = (f32[32,16,1024]{2,1,0:T(8,128)}, f32[32,16,1024]{2,1,0:T(8,128)}, u32[]{:S(2)}, u32[]{:S(2)}) collective-permute-start(f32[32,16,1024]{2,1,0:T(8,128)} %add.1214), channel_id=1, source_target_pairs={{0,8},{1,9},{2,10},{3,11},{4,12},{5,13},{6,14},{7,15},{8,0},{9,1},... | collective-permute-start | bytes 6291464 | tf_op jit(solution)/shard_map/ppermute | solution.py:14
  (82 other events, 2800.2 us)
